TPU v7x, 128 devices: a whole 4x4x4 slice. The times are simulated.
128 devices in a mesh: depth: 8 (over z, core), row: 16 (over y, x).
Axes of the slice: x: 4, y: 4, z: 4, core: 2. Of those that a mesh axis runs over, the one named last changes fastest.
Arguments:
- volume: float32 [384, 1024, 2048], P('depth', 'row'), may hold values from -6 to 6
- transfer: float32 [8], replicated, may hold values from 0.3 to 1.2
Outputs:
- image: float32 [4, 1024, 2048], P(None, 'row', 'depth')
All inputs are finite; a program needn't handle non-finite values.
Results may differ from a plain program's by a relative error of at most 0.0003.
Values sent between devices are 32-bit elements; how exact they have to be, the bound alone decides.
A program may use at most 192 MiB of HBM per device.

v0:
```python
import jax
import jax.numpy as jnp
from jax import lax
from jax.sharding import PartitionSpec as P


def with_halo(cells, sides, width):
    for axis, dim in sides:
        count = lax.axis_size(axis)
        ends = count - 1
        head = lax.slice_in_dim(cells, 0, width, axis=dim)
        tail = lax.slice_in_dim(cells, cells.shape[dim] - width, cells.shape[dim], axis=dim)
        cells = jnp.concatenate(
            [
                lax.ppermute(tail, axis, [(i, (i + 1) % count) for i in range(ends)]),
                cells,
                lax.ppermute(head, axis, [((i + 1) % count, i) for i in range(ends)]),
            ],
            axis=dim,
        )
    return cells


def slope_cols(center):
    zero_col = jnp.zeros_like(center[..., :1])
    right = jnp.concatenate([center[..., 1:], zero_col], -1)
    left = jnp.concatenate([zero_col, center[..., :-1]], -1)
    return 0.5 * (right - left)


def emit(framed, transfer, slices):
    center = framed[1:-1, 1:-1, :]
    slope_depth = 0.5 * (framed[2:, 1:-1, :] - framed[:-2, 1:-1, :])
    slope_row = 0.5 * (framed[1:-1, 2:, :] - framed[1:-1, :-2, :])
    slope_col = slope_cols(center)
    inverse = lax.rsqrt(
        slope_depth * slope_depth + slope_row * slope_row + slope_col * slope_col + 1.0
    )
    lambert = jnp.abs((slope_depth + 2.0 * slope_row + 2.0 * slope_col) * inverse) / 3.0
    ambient = 0.5 * transfer[7]
    shading = ambient + (1.0 - ambient) * lambert
    depth_term = 2.0 * transfer[6] / slices * jax.nn.softplus(center)
    opacity = -jnp.expm1(-depth_term)
    tinting = jax.nn.sigmoid(2.0 * center)
    weight = shading * opacity
    emitted = jnp.stack(
        [(transfer[channel] + transfer[3 + channel] * tinting) * weight for channel in range(3)]
    )
    return (emitted, depth_term)


def blend_parts(parts):
    depth_parts = parts[:, 3]
    before = jnp.cumsum(depth_parts, 0) - depth_parts
    color = jnp.sum(jnp.exp(-before)[:, None] * parts[:, :3], 0)
    total = jnp.sum(depth_parts, 0)
    return jnp.concatenate([color, total[None]], 0)


def on_device(volume, transfer):
    local_slices, local_rows, columns = volume.shape
    groups = lax.axis_size("depth")
    slices = local_slices * groups
    padded = with_halo(volume, (("depth", 0), ("row", 1)), 1)
    steps = local_slices // 8

    def march(carry, index):
        color, depth_acc = carry
        slab = lax.dynamic_slice_in_dim(padded, index * 8, 10, 0)
        emitted, depth_term = emit(slab, transfer, slices)
        before = jnp.cumsum(depth_term, 0) - depth_term
        passing = jnp.exp(-(depth_acc[None] + before))
        color = color + jnp.sum(passing[None] * emitted, 1)
        depth_acc = depth_acc + jnp.sum(depth_term, 0)
        return ((color, depth_acc), None)

    start_color = jnp.zeros((3, local_rows, columns), jnp.float32)
    start_depth = jnp.zeros((local_rows, columns), jnp.float32)
    (color, depth_acc), unused = lax.scan(
        march, (start_color, start_depth), jnp.arange(steps, dtype=jnp.int32)
    )
    partial_image = jnp.concatenate([color, depth_acc[None]], 0)
    final = blend_parts(
        lax.all_to_all(partial_image[None], "depth", split_axis=3, concat_axis=0, tiled=True)
    )
    return jnp.concatenate([final[:3], -jnp.expm1(-final[3:4])], 0)


def solution(mesh):
    in_specs = (P("depth", "row", None), P())
    out_specs = P(None, "row", "depth")
    return jax.shard_map(
        on_device, mesh=mesh, in_specs=in_specs, out_specs=out_specs, check_vma=False
    )
```

profile of v0, /device:TPU:14, one launch (start us, length us, event | category | flops | bytes accessed | tf_op | source)
XLA Modules:
  0.0 483.0 jit_solution(13706453914436330940)
XLA Ops:
  0.0 1.3 fusion.12
  1.3 1.8 collective-permute-start
  3.1 1.3 collective-permute-start.1
  4.6 10.6 %constant_dynamic-update-slice_fusion.1 = f32[50,64,2048]{2,1,0:T(8,128)S(1)} fusion(f32[50,64,2048]{2,1,0:T(8,128)S(1)} %constant_dynamic-update-slice_fusion.2, f32[48,64,2048]{2,1,0:T(8,128)} %param.4), kind=kLoop, calls=%fused_computation.28 | loop fusion | bytes 50331648
  15.3 0.8 fusion.11
  16.1 3.4 collective-permute-start.2
  19.5 4.4 copy-done.2
  24.0 2.7 collective-permute-start.3
  26.7 0.7 fusion.13
  28.7 7.4 %collective-permute-done.3 = f32[50,1,2048]{2,1,0:T(1,128)} collective-permute-done((f32[50,1,2048]{2,1,0:T(1,128)S(1)}, f32[50,1,2048]{2,1,0:T(1,128)}, u32[]{:S(2)}, u32[]{:S(2)}) %collective-permute-start.3) | collective-permute-done | bytes 409632 | tf_op jit(solution)/shard_map/ppermute | solution.py:17
  36.0 20.7 %pad_maximum_fusion = f32[50,66,2048]{2,1,0:T(8,128)} fusion(f32[50,1,2048]{2,1,0:T(1,128)} %collective-permute-done.3, f32[50,64,2048]{2,1,0:T(8,128)} %copy-done.2, f32[50,1,2048]{2,1,0:T(1,128)S(1)} %collective-permute-done.2), kind=kLoop, calls=%fused_computation.17 | loop fusion | flops 13516800 | bytes 54067200 | tf_op jit(solution)/shard_map/concatenate | solution.py:13
  56.7 343.4 %while.16 = (s32[]{:T(128)}, f32[3,64,2048]{2,1,0:T(8,128)S(1)}, f32[64,2048]{1,0:T(8,128)S(1)}, f32[]{:T(128)}, s32[6]{0:T(128)S(1)}, /*index=5*/f32[50,66,2048...) while((s32[]{:T(128)}, f32[3,64,2048]{2,1,0:T(8,128)S(1)}, ...), condition=%wide.region_4.5_spmd.clone, body=%wide.region_0.4_spmd.clone.sunk | while | flops 86507528 | bytes 139449296 | solution.py:79
  56.7 0.6 dynamic_slice.18
  57.8 8.3 %fusion.22 = (f32[8,64,2047]{2,1,0:T(8,128)}, f32[8,64,2047]{2,1,0:T(8,128)}) fusion(f32[50,66,2048]{2,1,0:T(8,128)} %get-tuple-element.322, s32[]{:T(128)S(6)} %add.257, s32[]{:T(128)S(6)} %add.258), kind=kLoop, calls=%fused_computation.31.clone.1 | loop fusion | bytes 16769032 | tf_op jit(solution)/shard_map/while/body/eval_jaxpr/slice | solution.py:26
  66.1 0.7 fusion.21
  66.7 18.1 %multiply_bitcast_fusion.5 = (f32[1,8,64,2048]{3,2,1,0:T(8,128)}, f32[8,64,2048]{2,1,0:T(8,128)S(1)}) fusion(f32[]{:T(128)} %bitcast.41, f32[]{:T(128)} %bitcast.42, f32[50,66,2048]{2,1,0:T(8,128)} %get-tuple-element.322, s32[]{:T(128)S(6)} %add.257, s32[]{:T(128)S(6)} %add.258, f32[]{:T(128)} %get-tuple-element.320, f32[]{:T(128)} %get-tuple-element.325, ...), kind=kLoop, calls=%fused_computation.9.clone.1 | loop fusion | flops 36700160 | bytes 37744680 | tf_op jit(solution)/shard_map/while/body/eval_jaxpr/stack | solution.py:46
  84.9 10.4 %multiply_bitcast_fusion.6 = (f32[1,8,64,2048]{3,2,1,0:T(8,128)}, f32[1,8,64,2048]{3,2,1,0:T(8,128)}, f32[64,2048]{1,0:T(8,128)S(1)}) fusion(f32[8,64,2048]{2,1,0:T(8,128)S(1)} %get-tuple-element.276, f32[]{:T(128)} %bitcast.44, f32[]{:T(128)} %bitcast.45, f32[50,66,2048]{2,1,0:T(8,128)} %get-tuple-element.322, s32[]{:T(128)S(6)} %add.257, ...), kind=kLoop, calls=%fused_computation.8.clone.1 | loop fusion | flops 18743296 | bytes 17301532 | tf_op jit(solution)/shard_map/while/body/eval_jaxpr/stack | solution.py:46
  95.5 12.9 %negate_exponential_fusion.3 = f32[8,64,2048]{2,1,0:T(8,128)S(1)} fusion(f32[64,2048]{1,0:T(8,128)S(1)} %get-tuple-element.285, f32[50,66,2048]{2,1,0:T(8,128)} %get-tuple-element.322, s32[]{:T(128)S(6)} %add.257, s32[]{:T(128)S(6)} %add.258, f32[]{:T(128)} %get-tuple-element.320), kind=kOutput, calls=%fused_computation.12.clone.1 | output fusion | flops 17825792 | bytes 8913416 | tf_op jit(solution)/shard_map/while/body/eval_jaxpr/jit(cumsum)/reduce_window_sum | solution.py:71
  108.4 4.0 fusion.24
  112.4 0.5 select_add_fusion.2
  112.9 0.6 dynamic_slice.18
  114.1 8.3 %fusion.22 = (f32[8,64,2047]{2,1,0:T(8,128)}, f32[8,64,2047]{2,1,0:T(8,128)}) fusion(f32[50,66,2048]{2,1,0:T(8,128)} %get-tuple-element.322, s32[]{:T(128)S(6)} %add.257, s32[]{:T(128)S(6)} %add.258), kind=kLoop, calls=%fused_computation.31.clone.1 | loop fusion | bytes 16769032 | tf_op jit(solution)/shard_map/while/body/eval_jaxpr/slice | solution.py:26
  122.3 0.7 fusion.21
  123.0 18.2 %multiply_bitcast_fusion.5 = (f32[1,8,64,2048]{3,2,1,0:T(8,128)}, f32[8,64,2048]{2,1,0:T(8,128)S(1)}) fusion(f32[]{:T(128)} %bitcast.41, f32[]{:T(128)} %bitcast.42, f32[50,66,2048]{2,1,0:T(8,128)} %get-tuple-element.322, s32[]{:T(128)S(6)} %add.257, s32[]{:T(128)S(6)} %add.258, f32[]{:T(128)} %get-tuple-element.320, f32[]{:T(128)} %get-tuple-element.325, ...), kind=kLoop, calls=%fused_computation.9.clone.1 | loop fusion | flops 36700160 | bytes 37744680 | tf_op jit(solution)/shard_map/while/body/eval_jaxpr/stack | solution.py:46
  141.2 10.4 %multiply_bitcast_fusion.6 = (f32[1,8,64,2048]{3,2,1,0:T(8,128)}, f32[1,8,64,2048]{3,2,1,0:T(8,128)}, f32[64,2048]{1,0:T(8,128)S(1)}) fusion(f32[8,64,2048]{2,1,0:T(8,128)S(1)} %get-tuple-element.276, f32[]{:T(128)} %bitcast.44, f32[]{:T(128)} %bitcast.45, f32[50,66,2048]{2,1,0:T(8,128)} %get-tuple-element.322, s32[]{:T(128)S(6)} %add.257, ...), kind=kLoop, calls=%fused_computation.8.clone.1 | loop fusion | flops 18743296 | bytes 17301532 | tf_op jit(solution)/shard_map/while/body/eval_jaxpr/stack | solution.py:46
  151.9 14.1 %negate_exponential_fusion.3 = f32[8,64,2048]{2,1,0:T(8,128)S(1)} fusion(f32[64,2048]{1,0:T(8,128)S(1)} %get-tuple-element.285, f32[50,66,2048]{2,1,0:T(8,128)} %get-tuple-element.322, s32[]{:T(128)S(6)} %add.257, s32[]{:T(128)S(6)} %add.258, f32[]{:T(128)} %get-tuple-element.320), kind=kOutput, calls=%fused_computation.12.clone.1 | output fusion | flops 17825792 | bytes 8913416 | tf_op jit(solution)/shard_map/while/body/eval_jaxpr/jit(cumsum)/reduce_window_sum | solution.py:71
  166.0 4.0 fusion.24
  170.5 0.6 dynamic_slice.18
  171.6 8.3 %fusion.22 = (f32[8,64,2047]{2,1,0:T(8,128)}, f32[8,64,2047]{2,1,0:T(8,128)}) fusion(f32[50,66,2048]{2,1,0:T(8,128)} %get-tuple-element.322, s32[]{:T(128)S(6)} %add.257, s32[]{:T(128)S(6)} %add.258), kind=kLoop, calls=%fused_computation.31.clone.1 | loop fusion | bytes 16769032 | tf_op jit(solution)/shard_map/while/body/eval_jaxpr/slice | solution.py:26
  179.9 0.7 fusion.21
  180.6 18.1 %multiply_bitcast_fusion.5 = (f32[1,8,64,2048]{3,2,1,0:T(8,128)}, f32[8,64,2048]{2,1,0:T(8,128)S(1)}) fusion(f32[]{:T(128)} %bitcast.41, f32[]{:T(128)} %bitcast.42, f32[50,66,2048]{2,1,0:T(8,128)} %get-tuple-element.322, s32[]{:T(128)S(6)} %add.257, s32[]{:T(128)S(6)} %add.258, f32[]{:T(128)} %get-tuple-element.320, f32[]{:T(128)} %get-tuple-element.325, ...), kind=kLoop, calls=%fused_computation.9.clone.1 | loop fusion | flops 36700160 | bytes 37744680 | tf_op jit(solution)/shard_map/while/body/eval_jaxpr/stack | solution.py:46
  198.7 10.4 %multiply_bitcast_fusion.6 = (f32[1,8,64,2048]{3,2,1,0:T(8,128)}, f32[1,8,64,2048]{3,2,1,0:T(8,128)}, f32[64,2048]{1,0:T(8,128)S(1)}) fusion(f32[8,64,2048]{2,1,0:T(8,128)S(1)} %get-tuple-element.276, f32[]{:T(128)} %bitcast.44, f32[]{:T(128)} %bitcast.45, f32[50,66,2048]{2,1,0:T(8,128)} %get-tuple-element.322, s32[]{:T(128)S(6)} %add.257, ...), kind=kLoop, calls=%fused_computation.8.clone.1 | loop fusion | flops 18743296 | bytes 17301532 | tf_op jit(solution)/shard_map/while/body/eval_jaxpr/stack | solution.py:46
  209.3 14.2 %negate_exponential_fusion.3 = f32[8,64,2048]{2,1,0:T(8,128)S(1)} fusion(f32[64,2048]{1,0:T(8,128)S(1)} %get-tuple-element.285, f32[50,66,2048]{2,1,0:T(8,128)} %get-tuple-element.322, s32[]{:T(128)S(6)} %add.257, s32[]{:T(128)S(6)} %add.258, f32[]{:T(128)} %get-tuple-element.320), kind=kOutput, calls=%fused_computation.12.clone.1 | output fusion | flops 17825792 | bytes 8913416 | tf_op jit(solution)/shard_map/while/body/eval_jaxpr/jit(cumsum)/reduce_window_sum | solution.py:71
  223.5 4.0 fusion.24
  228.0 0.6 dynamic_slice.18
  229.1 8.3 %fusion.22 = (f32[8,64,2047]{2,1,0:T(8,128)}, f32[8,64,2047]{2,1,0:T(8,128)}) fusion(f32[50,66,2048]{2,1,0:T(8,128)} %get-tuple-element.322, s32[]{:T(128)S(6)} %add.257, s32[]{:T(128)S(6)} %add.258), kind=kLoop, calls=%fused_computation.31.clone.1 | loop fusion | bytes 16769032 | tf_op jit(solution)/shard_map/while/body/eval_jaxpr/slice | solution.py:26
  237.4 0.7 fusion.21
  238.1 17.9 %multiply_bitcast_fusion.5 = (f32[1,8,64,2048]{3,2,1,0:T(8,128)}, f32[8,64,2048]{2,1,0:T(8,128)S(1)}) fusion(f32[]{:T(128)} %bitcast.41, f32[]{:T(128)} %bitcast.42, f32[50,66,2048]{2,1,0:T(8,128)} %get-tuple-element.322, s32[]{:T(128)S(6)} %add.257, s32[]{:T(128)S(6)} %add.258, f32[]{:T(128)} %get-tuple-element.320, f32[]{:T(128)} %get-tuple-element.325, ...), kind=kLoop, calls=%fused_computation.9.clone.1 | loop fusion | flops 36700160 | bytes 37744680 | tf_op jit(solution)/shard_map/while/body/eval_jaxpr/stack | solution.py:46
  256.0 10.4 %multiply_bitcast_fusion.6 = (f32[1,8,64,2048]{3,2,1,0:T(8,128)}, f32[1,8,64,2048]{3,2,1,0:T(8,128)}, f32[64,2048]{1,0:T(8,128)S(1)}) fusion(f32[8,64,2048]{2,1,0:T(8,128)S(1)} %get-tuple-element.276, f32[]{:T(128)} %bitcast.44, f32[]{:T(128)} %bitcast.45, f32[50,66,2048]{2,1,0:T(8,128)} %get-tuple-element.322, s32[]{:T(128)S(6)} %add.257, ...), kind=kLoop, calls=%fused_computation.8.clone.1 | loop fusion | flops 18743296 | bytes 17301532 | tf_op jit(solution)/shard_map/while/body/eval_jaxpr/stack | solution.py:46
  266.6 13.8 %negate_exponential_fusion.3 = f32[8,64,2048]{2,1,0:T(8,128)S(1)} fusion(f32[64,2048]{1,0:T(8,128)S(1)} %get-tuple-element.285, f32[50,66,2048]{2,1,0:T(8,128)} %get-tuple-element.322, s32[]{:T(128)S(6)} %add.257, s32[]{:T(128)S(6)} %add.258, f32[]{:T(128)} %get-tuple-element.320), kind=kOutput, calls=%fused_computation.12.clone.1 | output fusion | flops 17825792 | bytes 8913416 | tf_op jit(solution)/shard_map/while/body/eval_jaxpr/jit(cumsum)/reduce_window_sum | solution.py:71
  280.4 4.0 fusion.24
  285.0 0.6 dynamic_slice.18
  286.1 8.3 %fusion.22 = (f32[8,64,2047]{2,1,0:T(8,128)}, f32[8,64,2047]{2,1,0:T(8,128)}) fusion(f32[50,66,2048]{2,1,0:T(8,128)} %get-tuple-element.322, s32[]{:T(128)S(6)} %add.257, s32[]{:T(128)S(6)} %add.258), kind=kLoop, calls=%fused_computation.31.clone.1 | loop fusion | bytes 16769032 | tf_op jit(solution)/shard_map/while/body/eval_jaxpr/slice | solution.py:26
  294.4 0.7 fusion.21
  295.0 18.2 %multiply_bitcast_fusion.5 = (f32[1,8,64,2048]{3,2,1,0:T(8,128)}, f32[8,64,2048]{2,1,0:T(8,128)S(1)}) fusion(f32[]{:T(128)} %bitcast.41, f32[]{:T(128)} %bitcast.42, f32[50,66,2048]{2,1,0:T(8,128)} %get-tuple-element.322, s32[]{:T(128)S(6)} %add.257, s32[]{:T(128)S(6)} %add.258, f32[]{:T(128)} %get-tuple-element.320, f32[]{:T(128)} %get-tuple-element.325, ...), kind=kLoop, calls=%fused_computation.9.clone.1 | loop fusion | flops 36700160 | bytes 37744680 | tf_op jit(solution)/shard_map/while/body/eval_jaxpr/stack | solution.py:46
  313.3 10.4 %multiply_bitcast_fusion.6 = (f32[1,8,64,2048]{3,2,1,0:T(8,128)}, f32[1,8,64,2048]{3,2,1,0:T(8,128)}, f32[64,2048]{1,0:T(8,128)S(1)}) fusion(f32[8,64,2048]{2,1,0:T(8,128)S(1)} %get-tuple-element.276, f32[]{:T(128)} %bitcast.44, f32[]{:T(128)} %bitcast.45, f32[50,66,2048]{2,1,0:T(8,128)} %get-tuple-element.322, s32[]{:T(128)S(6)} %add.257, ...), kind=kLoop, calls=%fused_computation.8.clone.1 | loop fusion | flops 18743296 | bytes 17301532 | tf_op jit(solution)/shard_map/while/body/eval_jaxpr/stack | solution.py:46
  323.9 14.1 %negate_exponential_fusion.3 = f32[8,64,2048]{2,1,0:T(8,128)S(1)} fusion(f32[64,2048]{1,0:T(8,128)S(1)} %get-tuple-element.285, f32[50,66,2048]{2,1,0:T(8,128)} %get-tuple-element.322, s32[]{:T(128)S(6)} %add.257, s32[]{:T(128)S(6)} %add.258, f32[]{:T(128)} %get-tuple-element.320), kind=kOutput, calls=%fused_computation.12.clone.1 | output fusion | flops 17825792 | bytes 8913416 | tf_op jit(solution)/shard_map/while/body/eval_jaxpr/jit(cumsum)/reduce_window_sum | solution.py:71
  338.0 4.0 fusion.24
  342.6 0.6 dynamic_slice.18
  343.7 8.3 %fusion.22 = (f32[8,64,2047]{2,1,0:T(8,128)}, f32[8,64,2047]{2,1,0:T(8,128)}) fusion(f32[50,66,2048]{2,1,0:T(8,128)} %get-tuple-element.322, s32[]{:T(128)S(6)} %add.257, s32[]{:T(128)S(6)} %add.258), kind=kLoop, calls=%fused_computation.31.clone.1 | loop fusion | bytes 16769032 | tf_op jit(solution)/shard_map/while/body/eval_jaxpr/slice | solution.py:26
  351.9 0.7 fusion.21
  352.6 18.4 %multiply_bitcast_fusion.5 = (f32[1,8,64,2048]{3,2,1,0:T(8,128)}, f32[8,64,2048]{2,1,0:T(8,128)S(1)}) fusion(f32[]{:T(128)} %bitcast.41, f32[]{:T(128)} %bitcast.42, f32[50,66,2048]{2,1,0:T(8,128)} %get-tuple-element.322, s32[]{:T(128)S(6)} %add.257, s32[]{:T(128)S(6)} %add.258, f32[]{:T(128)} %get-tuple-element.320, f32[]{:T(128)} %get-tuple-element.325, ...), kind=kLoop, calls=%fused_computation.9.clone.1 | loop fusion | flops 36700160 | bytes 37744680 | tf_op jit(solution)/shard_map/while/body/eval_jaxpr/stack | solution.py:46
  371.0 10.4 %multiply_bitcast_fusion.6 = (f32[1,8,64,2048]{3,2,1,0:T(8,128)}, f32[1,8,64,2048]{3,2,1,0:T(8,128)}, f32[64,2048]{1,0:T(8,128)S(1)}) fusion(f32[8,64,2048]{2,1,0:T(8,128)S(1)} %get-tuple-element.276, f32[]{:T(128)} %bitcast.44, f32[]{:T(128)} %bitcast.45, f32[50,66,2048]{2,1,0:T(8,128)} %get-tuple-element.322, s32[]{:T(128)S(6)} %add.257, ...), kind=kLoop, calls=%fused_computation.8.clone.1 | loop fusion | flops 18743296 | bytes 17301532 | tf_op jit(solution)/shard_map/while/body/eval_jaxpr/stack | solution.py:46
  381.6 13.9 %negate_exponential_fusion.3 = f32[8,64,2048]{2,1,0:T(8,128)S(1)} fusion(f32[64,2048]{1,0:T(8,128)S(1)} %get-tuple-element.285, f32[50,66,2048]{2,1,0:T(8,128)} %get-tuple-element.322, s32[]{:T(128)S(6)} %add.257, s32[]{:T(128)S(6)} %add.258, f32[]{:T(128)} %get-tuple-element.320), kind=kOutput, calls=%fused_computation.12.clone.1 | output fusion | flops 17825792 | bytes 8913416 | tf_op jit(solution)/shard_map/while/body/eval_jaxpr/jit(cumsum)/reduce_window_sum | solution.py:71
  395.5 4.0 fusion.24
  400.0 3.1 copy.6
  403.5 5.3 %fusion.14 = f32[2048,1,4,64]{3,2,1,0:T(4,128)} fusion(f32[1,64,2048]{1,0,2:T(1,128)S(1)} %bitcast.50, f32[3,64,2048]{1,0,2:T(4,128)} %copy.6), kind=kLoop, calls=%fused_computation.36 | loop fusion | flops 524288 | bytes 4194304
  408.8 6.8 %reshape.30 = f32[8,1,65536]{2,1,0:T(1,128)S(1)} reshape(f32[2048,1,4,64]{3,2,1,0:T(4,128)} %fusion.14) | data formatting | bytes 4194304
  415.6 42.5 %all_to_all.18 = f32[8,1,65536]{2,1,0:T(1,128)} all-to-all(f32[8,1,65536]{2,1,0:T(1,128)S(1)} %reshape.30), channel_id=1, replica_groups=mesh['depth'=8,'row'=16] {'depth'}, dimensions={0} | all-to-all | bytes 4194304 | tf_op jit(solution)/shard_map/all_to_all | solution.py:84
  458.6 7.2 %reduce.1 = f32[8,65536]{1,0:T(8,128)S(1)} reduce(f32[8,1,65536]{2,1,0:T(1,128)} %all_to_all.18, f32[]{:T(128)} %broadcast.78), dimensions={1}, to_apply=%all_to_all.13.reduce_sub_computation | reduce | bytes 4194308 | tf_op jit(solution)/shard_map/all_to_all | solution.py:84
  465.8 4.8 reshape.31
  470.6 7.7 %negate_exponential_fusion.1 = (f32[8,1,64,256]{2,1,3,0:T(1,128)S(1)}, f32[64,256]{0,1:T(8,128)S(1)}) fusion(f32[8,4,64,256]{2,1,3,0:T(4,128)} %bitcast.48), kind=kOutput, calls=%fused_computation.21 | output fusion | flops 1294336 | bytes 2686976 | tf_op jit(solution)/shard_map/jit(cumsum)/reduce_window_sum | solution.py:54
  478.3 3.4 fusion.5
  482.1 0.9 copy.7
  (50 shorter events, 5.2 us)
Async XLA Ops:
  1.3 3.3 collective-permute-start
  3.1 12.2 %collective-permute-start.1 = (f32[1,64,2048]{2,1,0:T(8,128)S(1)}, f32[1,64,2048]{2,1,0:T(8,128)S(1)}, u32[]{:S(2)}, u32[]{:S(2)}) collective-permute-start(f32[1,64,2048]{2,1,0:T(8,128)S(1)} %get-tuple-element.196), channel_id=1, source_target_pairs={{16,0},{32,16},{48,32},{64,48},{80,64},{96,80},{112,96},{17,1},{33... | collective-permute-start | bytes 1572872 | tf_op jit(solution)/shard_map/ppermute | solution.py:17
  4.6 22.1 %copy-start.3 = (f32[8]{0:T(128)S(1)}, f32[8]{0:T(128)}, u32[]{:S(2)}) copy-start(f32[8]{0:T(128)} %param.5) | copy-start | bytes 100
  15.3 8.6 %copy-start.2 = (f32[50,64,2048]{2,1,0:T(8,128)}, f32[50,64,2048]{2,1,0:T(8,128)S(1)}, u32[]{:S(2)}) copy-start(f32[50,64,2048]{2,1,0:T(8,128)S(1)} %constant_dynamic-update-slice_fusion) | copy-start | bytes 78643200
  16.1 12.5 %collective-permute-start.2 = (f32[50,1,2048]{2,1,0:T(1,128)S(1)}, f32[50,1,2048]{2,1,0:T(1,128)S(1)}, u32[]{:S(2)}, u32[]{:S(2)}) collective-permute-start(f32[50,1,2048]{2,1,0:T(1,128)S(1)} %get-tuple-element.194), channel_id=1, source_target_pairs={{0,1},{1,2},{2,3},{3,4},{4,5},{5,6},{6,7},{7,8},{8,9},{9,10},{10,1... | collective-permute-start | bytes 1228808 | tf_op jit(solution)/shard_map/ppermute | solution.py:15
  24.0 12.0 %collective-permute-start.3 = (f32[50,1,2048]{2,1,0:T(1,128)S(1)}, f32[50,1,2048]{2,1,0:T(1,128)}, u32[]{:S(2)}, u32[]{:S(2)}) collective-permute-start(f32[50,1,2048]{2,1,0:T(1,128)S(1)} %get-tuple-element.195), channel_id=1, source_target_pairs={{1,0},{2,1},{3,2},{4,3},{5,4},{6,5},{7,6},{8,7},{9,8},{10,9},{11,1... | collective-permute-start | bytes 1228808 | tf_op jit(solution)/shard_map/ppermute | solution.py:17
  95.5 12.9 %copy-start = (f32[1,8,64,2048]{3,2,1,0:T(8,128)S(1)}, f32[1,8,64,2048]{3,2,1,0:T(8,128)}, u32[]{:S(2)}) copy-start(f32[1,8,64,2048]{3,2,1,0:T(8,128)} %get-tuple-element.283) | copy-start | bytes 12582916 | tf_op jit(solution)/shard_map/while
  95.5 12.9 %copy-start.1 = (f32[1,8,64,2048]{3,2,1,0:T(8,128)S(1)}, f32[1,8,64,2048]{3,2,1,0:T(8,128)}, u32[]{:S(2)}) copy-start(f32[1,8,64,2048]{3,2,1,0:T(8,128)} %get-tuple-element.282) | copy-start | bytes 12582916 | tf_op jit(solution)/shard_map/while
  151.8 14.1 %copy-start = (f32[1,8,64,2048]{3,2,1,0:T(8,128)S(1)}, f32[1,8,64,2048]{3,2,1,0:T(8,128)}, u32[]{:S(2)}) copy-start(f32[1,8,64,2048]{3,2,1,0:T(8,128)} %get-tuple-element.283) | copy-start | bytes 12582916 | tf_op jit(solution)/shard_map/while
  151.8 14.1 %copy-start.1 = (f32[1,8,64,2048]{3,2,1,0:T(8,128)S(1)}, f32[1,8,64,2048]{3,2,1,0:T(8,128)}, u32[]{:S(2)}) copy-start(f32[1,8,64,2048]{3,2,1,0:T(8,128)} %get-tuple-element.282) | copy-start | bytes 12582916 | tf_op jit(solution)/shard_map/while
  209.3 14.2 %copy-start = (f32[1,8,64,2048]{3,2,1,0:T(8,128)S(1)}, f32[1,8,64,2048]{3,2,1,0:T(8,128)}, u32[]{:S(2)}) copy-start(f32[1,8,64,2048]{3,2,1,0:T(8,128)} %get-tuple-element.283) | copy-start | bytes 12582916 | tf_op jit(solution)/shard_map/while
  209.3 14.2 %copy-start.1 = (f32[1,8,64,2048]{3,2,1,0:T(8,128)S(1)}, f32[1,8,64,2048]{3,2,1,0:T(8,128)}, u32[]{:S(2)}) copy-start(f32[1,8,64,2048]{3,2,1,0:T(8,128)} %get-tuple-element.282) | copy-start | bytes 12582916 | tf_op jit(solution)/shard_map/while
  266.6 13.8 %copy-start = (f32[1,8,64,2048]{3,2,1,0:T(8,128)S(1)}, f32[1,8,64,2048]{3,2,1,0:T(8,128)}, u32[]{:S(2)}) copy-start(f32[1,8,64,2048]{3,2,1,0:T(8,128)} %get-tuple-element.283) | copy-start | bytes 12582916 | tf_op jit(solution)/shard_map/while
  266.6 13.8 %copy-start.1 = (f32[1,8,64,2048]{3,2,1,0:T(8,128)S(1)}, f32[1,8,64,2048]{3,2,1,0:T(8,128)}, u32[]{:S(2)}) copy-start(f32[1,8,64,2048]{3,2,1,0:T(8,128)} %get-tuple-element.282) | copy-start | bytes 12582916 | tf_op jit(solution)/shard_map/while
  323.9 14.2 %copy-start = (f32[1,8,64,2048]{3,2,1,0:T(8,128)S(1)}, f32[1,8,64,2048]{3,2,1,0:T(8,128)}, u32[]{:S(2)}) copy-start(f32[1,8,64,2048]{3,2,1,0:T(8,128)} %get-tuple-element.283) | copy-start | bytes 12582916 | tf_op jit(solution)/shard_map/while
  323.9 14.2 %copy-start.1 = (f32[1,8,64,2048]{3,2,1,0:T(8,128)S(1)}, f32[1,8,64,2048]{3,2,1,0:T(8,128)}, u32[]{:S(2)}) copy-start(f32[1,8,64,2048]{3,2,1,0:T(8,128)} %get-tuple-element.282) | copy-start | bytes 12582916 | tf_op jit(solution)/shard_map/while
  381.6 13.9 %copy-start = (f32[1,8,64,2048]{3,2,1,0:T(8,128)S(1)}, f32[1,8,64,2048]{3,2,1,0:T(8,128)}, u32[]{:S(2)}) copy-start(f32[1,8,64,2048]{3,2,1,0:T(8,128)} %get-tuple-element.283) | copy-start | bytes 12582916 | tf_op jit(solution)/shard_map/while
  381.6 13.9 %copy-start.1 = (f32[1,8,64,2048]{3,2,1,0:T(8,128)S(1)}, f32[1,8,64,2048]{3,2,1,0:T(8,128)}, u32[]{:S(2)}) copy-start(f32[1,8,64,2048]{3,2,1,0:T(8,128)} %get-tuple-element.282) | copy-start | bytes 12582916 | tf_op jit(solution)/shard_map/while
where the time goes:
time: 484 us; the launch traced here: 483 us
  other arithmetic  327 us (68%)
  local copies, waits for them, and re-layouts  91.4 us (19%)
  blocking collectives  42.5 us (9%)
  starting transfers between devices  9.19 us (2%)
  waiting for transfers between devices  7.54 us (2%)
    another operation x12, other arithmetic, emit(): jnp.stack([(transfer[channel] + transfer[3 + channel] * tinting) * weight...  172 us
    another operation x6, other arithmetic, march(): before = jnp.cumsum(depth_term, 0) - depth_term  83 us
    slice x6, local copies, waits for them, and re-layouts, slope_cols(): right = jnp.concatenate([center[..., 1:], zero_col], -1)  49.7 us
    all_to_all x1, blocking collectives, on_device(): lax.all_to_all(partial_image[None], 'depth', split_axis=3, concat_axis=0,...  42.5 us
    unnamed x8, local copies, waits for them, and re-layouts  26.7 us
    reduce_sum x6, other arithmetic, march(): color = color + jnp.sum(passing[None] * emitted, 1)  23.7 us
    concatenate x1, other arithmetic, with_halo(): jnp.concatenate([lax.ppermute(tail, axis, [(i, (i + 1) % count) for i in...  20.7 us
  transfers between devices with their start and end apart: 4, of which 2 were waited for; matrix products, arithmetic and copies ran while one was open for 2% of the time, Pallas kernels for 0%

commit v1 on v0

--- a/solution.py
+++ b/solution.py
@@ -58,6 +58,16 @@
 
 
 def on_device(volume, transfer):
+
+    def _raise_packet(mine, mesh_name):
+        outer = lax.axis_size(mesh_name)
+        arr_now = jnp.split(mine, outer, 3)
+        e_now = lax.all_to_all(
+            jnp.stack(arr_now, 0), axis_name=mesh_name, split_axis=0, concat_axis=0
+        )
+        z = jnp.concatenate(e_now, 0)
+        return z
+
     local_slices, local_rows, columns = volume.shape
     groups = lax.axis_size("depth")
     slices = local_slices * groups
@@ -80,9 +90,7 @@
         march, (start_color, start_depth), jnp.arange(steps, dtype=jnp.int32)
     )
     partial_image = jnp.concatenate([color, depth_acc[None]], 0)
-    final = blend_parts(
-        lax.all_to_all(partial_image[None], "depth", split_axis=3, concat_axis=0, tiled=True)
-    )
+    final = blend_parts(_raise_packet(partial_image[None], mesh_name="depth"))
     return jnp.concatenate([final[:3], -jnp.expm1(-final[3:4])], 0)
 
 

time: 484 us -> 445 us (0.919)
  other arithmetic: 327 us -> 304 us
  local copies, waits for them, and re-layouts: 91.4 us -> 75.1 us
    unnamed x8 -> x13, local copies, waits for them, and re-layouts: 26.7 us -> 15.3 us
    another operation x1, other arithmetic: 7.68 us -> 0.12 us  [blend_parts(): before = jnp.cumsum(depth_parts, 0) - depth_parts]
    all_to_all x1 -> x0, other arithmetic: 7.22 us -> none  [on_device(): lax.all_to_all(partial_image[None], 'depth', split_axis=3, concat_axis=0,...]
    unnamed x3 -> x2, other arithmetic: 5.27 us -> 0.01 us
  transfers between devices with their start and end apart: 4 -> 4, of which waited for: 2 -> 2; matrix products, arithmetic and copies ran while one was open for 2% -> 3% of each run, Pallas kernels for 0% -> 0%
where the time goes in v1:
time: 445 us; the launch traced here: 444 us
  other arithmetic  304 us (68%)
  local copies, waits for them, and re-layouts  75.1 us (17%)
  blocking collectives  42.4 us (10%)
  starting transfers between devices  9.19 us (2%)
  waiting for transfers between devices  7.54 us (2%)
    another operation x12, other arithmetic, emit(): jnp.stack([(transfer[channel] + transfer[3 + channel] * tinting) * weight...  172 us
    another operation x6, other arithmetic, march(): before = jnp.cumsum(depth_term, 0) - depth_term  83 us
    slice x6, local copies, waits for them, and re-layouts, slope_cols(): right = jnp.concatenate([center[..., 1:], zero_col], -1)  49.7 us
    all_to_all x1, blocking collectives, _raise_packet(): lax.all_to_all(jnp.stack(arr_now, 0), axis_name=mesh_name, split_axis=0,...  42.4 us
    reduce_sum x6, other arithmetic, march(): color = color + jnp.sum(passing[None] * emitted, 1)  23.7 us
    concatenate x1, other arithmetic, with_halo(): jnp.concatenate([lax.ppermute(tail, axis, [(i, (i + 1) % count) for i in...  20.7 us
    unnamed x13, local copies, waits for them, and re-layouts  15.3 us
  transfers between devices with their start and end apart: 4, of which 2 were waited for; matrix products, arithmetic and copies ran while one was open for 3% of the time, Pallas kernels for 0%

profile of v1, /device:TPU:14, one launch (start us, length us, event | category | flops | bytes accessed | tf_op | source)
XLA Modules:
  0.0 443.9 jit_solution(1621244166054510542)
XLA Ops:
  0.0 1.3 fusion.22
  1.3 1.8 collective-permute-start
  3.1 1.3 collective-permute-start.1
  4.4 0.2 collective-permute-done
  4.6 10.6 %constant_dynamic-update-slice_fusion.1 = f32[50,64,2048]{2,1,0:T(8,128)S(1)} fusion(f32[50,64,2048]{2,1,0:T(8,128)S(1)} %constant_dynamic-update-slice_fusion.2, f32[48,64,2048]{2,1,0:T(8,128)} %param.4), kind=kLoop, calls=%fused_computation.46 | loop fusion | bytes 50331648
  15.3 0.8 fusion.21
  16.1 3.4 collective-permute-start.2
  19.5 4.4 %copy-done.2 = f32[50,64,2048]{2,1,0:T(8,128)} copy-done((f32[50,64,2048]{2,1,0:T(8,128)}, f32[50,64,2048]{2,1,0:T(8,128)S(1)}, u32[]{:S(2)}) %copy-start.2) | copy-done | bytes 26214424
  24.0 2.7 collective-permute-start.3
  26.7 0.7 fusion.23
  28.7 7.4 %collective-permute-done.3 = f32[50,1,2048]{2,1,0:T(1,128)} collective-permute-done((f32[50,1,2048]{2,1,0:T(1,128)S(1)}, f32[50,1,2048]{2,1,0:T(1,128)}, u32[]{:S(2)}, u32[]{:S(2)}) %collective-permute-start.3) | collective-permute-done | bytes 409632 | tf_op jit(solution)/shard_map/ppermute | solution.py:17
  36.0 20.7 %pad_maximum_fusion = f32[50,66,2048]{2,1,0:T(8,128)} fusion(f32[50,1,2048]{2,1,0:T(1,128)} %collective-permute-done.3, f32[50,64,2048]{2,1,0:T(8,128)} %copy-done.2, f32[50,1,2048]{2,1,0:T(1,128)S(1)} %collective-permute-done.2), kind=kLoop, calls=%fused_computation.17 | loop fusion | flops 13516800 | bytes 54067200 | tf_op jit(solution)/shard_map/concatenate | solution.py:13
  56.7 343.4 %while.16 = (s32[]{:T(128)}, f32[3,64,2048]{2,1,0:T(8,128)S(1)}, f32[64,2048]{1,0:T(8,128)S(1)}, f32[]{:T(128)}, s32[6]{0:T(128)S(1)}, /*index=5*/f32[50,66,2048...) while((s32[]{:T(128)}, f32[3,64,2048]{2,1,0:T(8,128)S(1)}, ...), condition=%wide.region_4.5_spmd.clone, body=%wide.region_0.4_spmd.clone.sunk | while | flops 86507528 | bytes 139449296 | solution.py:89
  56.7 0.6 dynamic_slice.18
  57.8 8.3 %fusion.31 = (f32[8,64,2047]{2,1,0:T(8,128)}, f32[8,64,2047]{2,1,0:T(8,128)}) fusion(f32[50,66,2048]{2,1,0:T(8,128)} %get-tuple-element.320, s32[]{:T(128)S(6)} %add.256, s32[]{:T(128)S(6)} %add.257), kind=kLoop, calls=%fused_computation.49.clone.1 | loop fusion | bytes 16769032 | tf_op jit(solution)/shard_map/while/body/eval_jaxpr/slice | solution.py:26
  66.1 0.7 fusion.30
  66.7 18.1 %multiply_bitcast_fusion.5 = (f32[1,8,64,2048]{3,2,1,0:T(8,128)}, f32[8,64,2048]{2,1,0:T(8,128)S(1)}) fusion(f32[]{:T(128)} %bitcast.66, f32[]{:T(128)} %bitcast.67, f32[50,66,2048]{2,1,0:T(8,128)} %get-tuple-element.320, s32[]{:T(128)S(6)} %add.256, s32[]{:T(128)S(6)} %add.257, f32[]{:T(128)} %get-tuple-element.318, f32[]{:T(128)} %get-tuple-element.323, ...), kind=kLoop, calls=%fused_computation.9.clone.1 | loop fusion | flops 36700160 | bytes 37744680 | tf_op jit(solution)/shard_map/while/body/eval_jaxpr/stack | solution.py:46
  84.9 10.4 %multiply_bitcast_fusion.6 = (f32[1,8,64,2048]{3,2,1,0:T(8,128)}, f32[1,8,64,2048]{3,2,1,0:T(8,128)}, f32[64,2048]{1,0:T(8,128)S(1)}) fusion(f32[8,64,2048]{2,1,0:T(8,128)S(1)} %get-tuple-element.274, f32[]{:T(128)} %bitcast.69, f32[]{:T(128)} %bitcast.70, f32[50,66,2048]{2,1,0:T(8,128)} %get-tuple-element.320, s32[]{:T(128)S(6)} %add.256, ...), kind=kLoop, calls=%fused_computation.8.clone.1 | loop fusion | flops 18743296 | bytes 17301532 | tf_op jit(solution)/shard_map/while/body/eval_jaxpr/stack | solution.py:46
  95.5 12.9 %negate_exponential_fusion.2 = f32[8,64,2048]{2,1,0:T(8,128)S(1)} fusion(f32[64,2048]{1,0:T(8,128)S(1)} %get-tuple-element.283, f32[50,66,2048]{2,1,0:T(8,128)} %get-tuple-element.320, s32[]{:T(128)S(6)} %add.256, s32[]{:T(128)S(6)} %add.257, f32[]{:T(128)} %get-tuple-element.318), kind=kOutput, calls=%fused_computation.12.clone.1 | output fusion | flops 17825792 | bytes 8913416 | tf_op jit(solution)/shard_map/while/body/eval_jaxpr/jit(cumsum)/reduce_window_sum | solution.py:81
  108.4 4.0 fusion.33
  112.4 0.5 select_add_fusion.2
  112.9 0.6 dynamic_slice.18
  114.1 8.3 %fusion.31 = (f32[8,64,2047]{2,1,0:T(8,128)}, f32[8,64,2047]{2,1,0:T(8,128)}) fusion(f32[50,66,2048]{2,1,0:T(8,128)} %get-tuple-element.320, s32[]{:T(128)S(6)} %add.256, s32[]{:T(128)S(6)} %add.257), kind=kLoop, calls=%fused_computation.49.clone.1 | loop fusion | bytes 16769032 | tf_op jit(solution)/shard_map/while/body/eval_jaxpr/slice | solution.py:26
  122.3 0.7 fusion.30
  123.0 18.2 %multiply_bitcast_fusion.5 = (f32[1,8,64,2048]{3,2,1,0:T(8,128)}, f32[8,64,2048]{2,1,0:T(8,128)S(1)}) fusion(f32[]{:T(128)} %bitcast.66, f32[]{:T(128)} %bitcast.67, f32[50,66,2048]{2,1,0:T(8,128)} %get-tuple-element.320, s32[]{:T(128)S(6)} %add.256, s32[]{:T(128)S(6)} %add.257, f32[]{:T(128)} %get-tuple-element.318, f32[]{:T(128)} %get-tuple-element.323, ...), kind=kLoop, calls=%fused_computation.9.clone.1 | loop fusion | flops 36700160 | bytes 37744680 | tf_op jit(solution)/shard_map/while/body/eval_jaxpr/stack | solution.py:46
  141.2 10.4 %multiply_bitcast_fusion.6 = (f32[1,8,64,2048]{3,2,1,0:T(8,128)}, f32[1,8,64,2048]{3,2,1,0:T(8,128)}, f32[64,2048]{1,0:T(8,128)S(1)}) fusion(f32[8,64,2048]{2,1,0:T(8,128)S(1)} %get-tuple-element.274, f32[]{:T(128)} %bitcast.69, f32[]{:T(128)} %bitcast.70, f32[50,66,2048]{2,1,0:T(8,128)} %get-tuple-element.320, s32[]{:T(128)S(6)} %add.256, ...), kind=kLoop, calls=%fused_computation.8.clone.1 | loop fusion | flops 18743296 | bytes 17301532 | tf_op jit(solution)/shard_map/while/body/eval_jaxpr/stack | solution.py:46
  151.9 14.1 %negate_exponential_fusion.2 = f32[8,64,2048]{2,1,0:T(8,128)S(1)} fusion(f32[64,2048]{1,0:T(8,128)S(1)} %get-tuple-element.283, f32[50,66,2048]{2,1,0:T(8,128)} %get-tuple-element.320, s32[]{:T(128)S(6)} %add.256, s32[]{:T(128)S(6)} %add.257, f32[]{:T(128)} %get-tuple-element.318), kind=kOutput, calls=%fused_computation.12.clone.1 | output fusion | flops 17825792 | bytes 8913416 | tf_op jit(solution)/shard_map/while/body/eval_jaxpr/jit(cumsum)/reduce_window_sum | solution.py:81
  166.0 4.0 fusion.33
  169.9 0.5 select_add_fusion.2
  170.5 0.6 dynamic_slice.18
  171.6 8.3 %fusion.31 = (f32[8,64,2047]{2,1,0:T(8,128)}, f32[8,64,2047]{2,1,0:T(8,128)}) fusion(f32[50,66,2048]{2,1,0:T(8,128)} %get-tuple-element.320, s32[]{:T(128)S(6)} %add.256, s32[]{:T(128)S(6)} %add.257), kind=kLoop, calls=%fused_computation.49.clone.1 | loop fusion | bytes 16769032 | tf_op jit(solution)/shard_map/while/body/eval_jaxpr/slice | solution.py:26
  179.9 0.7 fusion.30
  180.6 18.1 %multiply_bitcast_fusion.5 = (f32[1,8,64,2048]{3,2,1,0:T(8,128)}, f32[8,64,2048]{2,1,0:T(8,128)S(1)}) fusion(f32[]{:T(128)} %bitcast.66, f32[]{:T(128)} %bitcast.67, f32[50,66,2048]{2,1,0:T(8,128)} %get-tuple-element.320, s32[]{:T(128)S(6)} %add.256, s32[]{:T(128)S(6)} %add.257, f32[]{:T(128)} %get-tuple-element.318, f32[]{:T(128)} %get-tuple-element.323, ...), kind=kLoop, calls=%fused_computation.9.clone.1 | loop fusion | flops 36700160 | bytes 37744680 | tf_op jit(solution)/shard_map/while/body/eval_jaxpr/stack | solution.py:46
  198.7 10.4 %multiply_bitcast_fusion.6 = (f32[1,8,64,2048]{3,2,1,0:T(8,128)}, f32[1,8,64,2048]{3,2,1,0:T(8,128)}, f32[64,2048]{1,0:T(8,128)S(1)}) fusion(f32[8,64,2048]{2,1,0:T(8,128)S(1)} %get-tuple-element.274, f32[]{:T(128)} %bitcast.69, f32[]{:T(128)} %bitcast.70, f32[50,66,2048]{2,1,0:T(8,128)} %get-tuple-element.320, s32[]{:T(128)S(6)} %add.256, ...), kind=kLoop, calls=%fused_computation.8.clone.1 | loop fusion | flops 18743296 | bytes 17301532 | tf_op jit(solution)/shard_map/while/body/eval_jaxpr/stack | solution.py:46
  209.3 14.2 %negate_exponential_fusion.2 = f32[8,64,2048]{2,1,0:T(8,128)S(1)} fusion(f32[64,2048]{1,0:T(8,128)S(1)} %get-tuple-element.283, f32[50,66,2048]{2,1,0:T(8,128)} %get-tuple-element.320, s32[]{:T(128)S(6)} %add.256, s32[]{:T(128)S(6)} %add.257, f32[]{:T(128)} %get-tuple-element.318), kind=kOutput, calls=%fused_computation.12.clone.1 | output fusion | flops 17825792 | bytes 8913416 | tf_op jit(solution)/shard_map/while/body/eval_jaxpr/jit(cumsum)/reduce_window_sum | solution.py:81
  223.5 4.0 fusion.33
  227.4 0.5 select_add_fusion.2
  228.0 0.6 dynamic_slice.18
  229.1 8.3 %fusion.31 = (f32[8,64,2047]{2,1,0:T(8,128)}, f32[8,64,2047]{2,1,0:T(8,128)}) fusion(f32[50,66,2048]{2,1,0:T(8,128)} %get-tuple-element.320, s32[]{:T(128)S(6)} %add.256, s32[]{:T(128)S(6)} %add.257), kind=kLoop, calls=%fused_computation.49.clone.1 | loop fusion | bytes 16769032 | tf_op jit(solution)/shard_map/while/body/eval_jaxpr/slice | solution.py:26
  237.4 0.7 fusion.30
  238.1 17.9 %multiply_bitcast_fusion.5 = (f32[1,8,64,2048]{3,2,1,0:T(8,128)}, f32[8,64,2048]{2,1,0:T(8,128)S(1)}) fusion(f32[]{:T(128)} %bitcast.66, f32[]{:T(128)} %bitcast.67, f32[50,66,2048]{2,1,0:T(8,128)} %get-tuple-element.320, s32[]{:T(128)S(6)} %add.256, s32[]{:T(128)S(6)} %add.257, f32[]{:T(128)} %get-tuple-element.318, f32[]{:T(128)} %get-tuple-element.323, ...), kind=kLoop, calls=%fused_computation.9.clone.1 | loop fusion | flops 36700160 | bytes 37744680 | tf_op jit(solution)/shard_map/while/body/eval_jaxpr/stack | solution.py:46
  256.0 10.4 %multiply_bitcast_fusion.6 = (f32[1,8,64,2048]{3,2,1,0:T(8,128)}, f32[1,8,64,2048]{3,2,1,0:T(8,128)}, f32[64,2048]{1,0:T(8,128)S(1)}) fusion(f32[8,64,2048]{2,1,0:T(8,128)S(1)} %get-tuple-element.274, f32[]{:T(128)} %bitcast.69, f32[]{:T(128)} %bitcast.70, f32[50,66,2048]{2,1,0:T(8,128)} %get-tuple-element.320, s32[]{:T(128)S(6)} %add.256, ...), kind=kLoop, calls=%fused_computation.8.clone.1 | loop fusion | flops 18743296 | bytes 17301532 | tf_op jit(solution)/shard_map/while/body/eval_jaxpr/stack | solution.py:46
  266.6 13.8 %negate_exponential_fusion.2 = f32[8,64,2048]{2,1,0:T(8,128)S(1)} fusion(f32[64,2048]{1,0:T(8,128)S(1)} %get-tuple-element.283, f32[50,66,2048]{2,1,0:T(8,128)} %get-tuple-element.320, s32[]{:T(128)S(6)} %add.256, s32[]{:T(128)S(6)} %add.257, f32[]{:T(128)} %get-tuple-element.318), kind=kOutput, calls=%fused_computation.12.clone.1 | output fusion | flops 17825792 | bytes 8913416 | tf_op jit(solution)/shard_map/while/body/eval_jaxpr/jit(cumsum)/reduce_window_sum | solution.py:81
  280.4 4.0 fusion.33
  284.4 0.5 select_add_fusion.2
  285.0 0.6 dynamic_slice.18
  286.1 8.3 %fusion.31 = (f32[8,64,2047]{2,1,0:T(8,128)}, f32[8,64,2047]{2,1,0:T(8,128)}) fusion(f32[50,66,2048]{2,1,0:T(8,128)} %get-tuple-element.320, s32[]{:T(128)S(6)} %add.256, s32[]{:T(128)S(6)} %add.257), kind=kLoop, calls=%fused_computation.49.clone.1 | loop fusion | bytes 16769032 | tf_op jit(solution)/shard_map/while/body/eval_jaxpr/slice | solution.py:26
  294.4 0.7 fusion.30
  295.0 18.2 %multiply_bitcast_fusion.5 = (f32[1,8,64,2048]{3,2,1,0:T(8,128)}, f32[8,64,2048]{2,1,0:T(8,128)S(1)}) fusion(f32[]{:T(128)} %bitcast.66, f32[]{:T(128)} %bitcast.67, f32[50,66,2048]{2,1,0:T(8,128)} %get-tuple-element.320, s32[]{:T(128)S(6)} %add.256, s32[]{:T(128)S(6)} %add.257, f32[]{:T(128)} %get-tuple-element.318, f32[]{:T(128)} %get-tuple-element.323, ...), kind=kLoop, calls=%fused_computation.9.clone.1 | loop fusion | flops 36700160 | bytes 37744680 | tf_op jit(solution)/shard_map/while/body/eval_jaxpr/stack | solution.py:46
  313.3 10.4 %multiply_bitcast_fusion.6 = (f32[1,8,64,2048]{3,2,1,0:T(8,128)}, f32[1,8,64,2048]{3,2,1,0:T(8,128)}, f32[64,2048]{1,0:T(8,128)S(1)}) fusion(f32[8,64,2048]{2,1,0:T(8,128)S(1)} %get-tuple-element.274, f32[]{:T(128)} %bitcast.69, f32[]{:T(128)} %bitcast.70, f32[50,66,2048]{2,1,0:T(8,128)} %get-tuple-element.320, s32[]{:T(128)S(6)} %add.256, ...), kind=kLoop, calls=%fused_computation.8.clone.1 | loop fusion | flops 18743296 | bytes 17301532 | tf_op jit(solution)/shard_map/while/body/eval_jaxpr/stack | solution.py:46
  323.9 14.1 %negate_exponential_fusion.2 = f32[8,64,2048]{2,1,0:T(8,128)S(1)} fusion(f32[64,2048]{1,0:T(8,128)S(1)} %get-tuple-element.283, f32[50,66,2048]{2,1,0:T(8,128)} %get-tuple-element.320, s32[]{:T(128)S(6)} %add.256, s32[]{:T(128)S(6)} %add.257, f32[]{:T(128)} %get-tuple-element.318), kind=kOutput, calls=%fused_computation.12.clone.1 | output fusion | flops 17825792 | bytes 8913416 | tf_op jit(solution)/shard_map/while/body/eval_jaxpr/jit(cumsum)/reduce_window_sum | solution.py:81
  338.0 4.0 fusion.33
  342.0 0.5 select_add_fusion.2
  342.6 0.6 dynamic_slice.18
  343.7 8.3 %fusion.31 = (f32[8,64,2047]{2,1,0:T(8,128)}, f32[8,64,2047]{2,1,0:T(8,128)}) fusion(f32[50,66,2048]{2,1,0:T(8,128)} %get-tuple-element.320, s32[]{:T(128)S(6)} %add.256, s32[]{:T(128)S(6)} %add.257), kind=kLoop, calls=%fused_computation.49.clone.1 | loop fusion | bytes 16769032 | tf_op jit(solution)/shard_map/while/body/eval_jaxpr/slice | solution.py:26
  351.9 0.7 fusion.30
  352.6 18.4 %multiply_bitcast_fusion.5 = (f32[1,8,64,2048]{3,2,1,0:T(8,128)}, f32[8,64,2048]{2,1,0:T(8,128)S(1)}) fusion(f32[]{:T(128)} %bitcast.66, f32[]{:T(128)} %bitcast.67, f32[50,66,2048]{2,1,0:T(8,128)} %get-tuple-element.320, s32[]{:T(128)S(6)} %add.256, s32[]{:T(128)S(6)} %add.257, f32[]{:T(128)} %get-tuple-element.318, f32[]{:T(128)} %get-tuple-element.323, ...), kind=kLoop, calls=%fused_computation.9.clone.1 | loop fusion | flops 36700160 | bytes 37744680 | tf_op jit(solution)/shard_map/while/body/eval_jaxpr/stack | solution.py:46
  371.0 10.4 %multiply_bitcast_fusion.6 = (f32[1,8,64,2048]{3,2,1,0:T(8,128)}, f32[1,8,64,2048]{3,2,1,0:T(8,128)}, f32[64,2048]{1,0:T(8,128)S(1)}) fusion(f32[8,64,2048]{2,1,0:T(8,128)S(1)} %get-tuple-element.274, f32[]{:T(128)} %bitcast.69, f32[]{:T(128)} %bitcast.70, f32[50,66,2048]{2,1,0:T(8,128)} %get-tuple-element.320, s32[]{:T(128)S(6)} %add.256, ...), kind=kLoop, calls=%fused_computation.8.clone.1 | loop fusion | flops 18743296 | bytes 17301532 | tf_op jit(solution)/shard_map/while/body/eval_jaxpr/stack | solution.py:46
  381.6 13.9 %negate_exponential_fusion.2 = f32[8,64,2048]{2,1,0:T(8,128)S(1)} fusion(f32[64,2048]{1,0:T(8,128)S(1)} %get-tuple-element.283, f32[50,66,2048]{2,1,0:T(8,128)} %get-tuple-element.320, s32[]{:T(128)S(6)} %add.256, s32[]{:T(128)S(6)} %add.257, f32[]{:T(128)} %get-tuple-element.318), kind=kOutput, calls=%fused_computation.12.clone.1 | output fusion | flops 17825792 | bytes 8913416 | tf_op jit(solution)/shard_map/while/body/eval_jaxpr/jit(cumsum)/reduce_window_sum | solution.py:81
  395.5 4.0 fusion.33
  399.5 0.5 select_add_fusion.2
  400.0 0.2 maximum_bitcast_fusion
  400.5 42.4 %all_to_all.5 = f32[8,1,4,64,256]{4,3,2,1,0:T(8,128)S(1)} all-to-all(f32[8,1,4,64,256]{4,3,2,1,0:T(8,128)S(1)} %fusion.10), channel_id=1, replica_groups=mesh['depth'=8,'row'=16] {'depth'}, dimensions={0} | all-to-all | bytes 4194304 | tf_op jit(solution)/shard_map/all_to_all | solution.py:65
  443.2 0.7 pad_maximum_fusion.1
  (52 shorter events, 1.6 us)
Async XLA Ops:
  1.3 3.3 collective-permute-start
  3.1 12.2 %collective-permute-start.1 = (f32[1,64,2048]{2,1,0:T(8,128)S(1)}, f32[1,64,2048]{2,1,0:T(8,128)S(1)}, u32[]{:S(2)}, u32[]{:S(2)}) collective-permute-start(f32[1,64,2048]{2,1,0:T(8,128)S(1)} %get-tuple-element.196), channel_id=1, source_target_pairs={{16,0},{32,16},{48,32},{64,48},{80,64},{96,80},{112,96},{17,1},{33... | collective-permute-start | bytes 1572872 | tf_op jit(solution)/shard_map/ppermute | solution.py:17
  4.6 22.1 %copy-start.3 = (f32[8]{0:T(128)S(1)}, f32[8]{0:T(128)}, u32[]{:S(2)}) copy-start(f32[8]{0:T(128)} %param.5) | copy-start | bytes 100
  15.3 8.6 %copy-start.2 = (f32[50,64,2048]{2,1,0:T(8,128)}, f32[50,64,2048]{2,1,0:T(8,128)S(1)}, u32[]{:S(2)}) copy-start(f32[50,64,2048]{2,1,0:T(8,128)S(1)} %constant_dynamic-update-slice_fusion) | copy-start | bytes 78643200
  16.1 12.5 %collective-permute-start.2 = (f32[50,1,2048]{2,1,0:T(1,128)S(1)}, f32[50,1,2048]{2,1,0:T(1,128)S(1)}, u32[]{:S(2)}, u32[]{:S(2)}) collective-permute-start(f32[50,1,2048]{2,1,0:T(1,128)S(1)} %get-tuple-element.194), channel_id=1, source_target_pairs={{0,1},{1,2},{2,3},{3,4},{4,5},{5,6},{6,7},{7,8},{8,9},{9,10},{10,1... | collective-permute-start | bytes 1228808 | tf_op jit(solution)/shard_map/ppermute | solution.py:15
  24.0 12.0 %collective-permute-start.3 = (f32[50,1,2048]{2,1,0:T(1,128)S(1)}, f32[50,1,2048]{2,1,0:T(1,128)}, u32[]{:S(2)}, u32[]{:S(2)}) collective-permute-start(f32[50,1,2048]{2,1,0:T(1,128)S(1)} %get-tuple-element.195), channel_id=1, source_target_pairs={{1,0},{2,1},{3,2},{4,3},{5,4},{6,5},{7,6},{8,7},{9,8},{10,9},{11,1... | collective-permute-start | bytes 1228808 | tf_op jit(solution)/shard_map/ppermute | solution.py:17
  95.5 12.9 %copy-start = (f32[1,8,64,2048]{3,2,1,0:T(8,128)S(1)}, f32[1,8,64,2048]{3,2,1,0:T(8,128)}, u32[]{:S(2)}) copy-start(f32[1,8,64,2048]{3,2,1,0:T(8,128)} %get-tuple-element.281) | copy-start | bytes 12582916 | tf_op jit(solution)/shard_map/while
  95.5 12.9 %copy-start.1 = (f32[1,8,64,2048]{3,2,1,0:T(8,128)S(1)}, f32[1,8,64,2048]{3,2,1,0:T(8,128)}, u32[]{:S(2)}) copy-start(f32[1,8,64,2048]{3,2,1,0:T(8,128)} %get-tuple-element.280) | copy-start | bytes 12582916 | tf_op jit(solution)/shard_map/while
  151.8 14.1 %copy-start = (f32[1,8,64,2048]{3,2,1,0:T(8,128)S(1)}, f32[1,8,64,2048]{3,2,1,0:T(8,128)}, u32[]{:S(2)}) copy-start(f32[1,8,64,2048]{3,2,1,0:T(8,128)} %get-tuple-element.281) | copy-start | bytes 12582916 | tf_op jit(solution)/shard_map/while
  151.8 14.1 %copy-start.1 = (f32[1,8,64,2048]{3,2,1,0:T(8,128)S(1)}, f32[1,8,64,2048]{3,2,1,0:T(8,128)}, u32[]{:S(2)}) copy-start(f32[1,8,64,2048]{3,2,1,0:T(8,128)} %get-tuple-element.280) | copy-start | bytes 12582916 | tf_op jit(solution)/shard_map/while
  209.3 14.2 %copy-start = (f32[1,8,64,2048]{3,2,1,0:T(8,128)S(1)}, f32[1,8,64,2048]{3,2,1,0:T(8,128)}, u32[]{:S(2)}) copy-start(f32[1,8,64,2048]{3,2,1,0:T(8,128)} %get-tuple-element.281) | copy-start | bytes 12582916 | tf_op jit(solution)/shard_map/while
  209.3 14.2 %copy-start.1 = (f32[1,8,64,2048]{3,2,1,0:T(8,128)S(1)}, f32[1,8,64,2048]{3,2,1,0:T(8,128)}, u32[]{:S(2)}) copy-start(f32[1,8,64,2048]{3,2,1,0:T(8,128)} %get-tuple-element.280) | copy-start | bytes 12582916 | tf_op jit(solution)/shard_map/while
  266.6 13.8 %copy-start = (f32[1,8,64,2048]{3,2,1,0:T(8,128)S(1)}, f32[1,8,64,2048]{3,2,1,0:T(8,128)}, u32[]{:S(2)}) copy-start(f32[1,8,64,2048]{3,2,1,0:T(8,128)} %get-tuple-element.281) | copy-start | bytes 12582916 | tf_op jit(solution)/shard_map/while
  266.6 13.8 %copy-start.1 = (f32[1,8,64,2048]{3,2,1,0:T(8,128)S(1)}, f32[1,8,64,2048]{3,2,1,0:T(8,128)}, u32[]{:S(2)}) copy-start(f32[1,8,64,2048]{3,2,1,0:T(8,128)} %get-tuple-element.280) | copy-start | bytes 12582916 | tf_op jit(solution)/shard_map/while
  323.9 14.2 %copy-start = (f32[1,8,64,2048]{3,2,1,0:T(8,128)S(1)}, f32[1,8,64,2048]{3,2,1,0:T(8,128)}, u32[]{:S(2)}) copy-start(f32[1,8,64,2048]{3,2,1,0:T(8,128)} %get-tuple-element.281) | copy-start | bytes 12582916 | tf_op jit(solution)/shard_map/while
  323.9 14.2 %copy-start.1 = (f32[1,8,64,2048]{3,2,1,0:T(8,128)S(1)}, f32[1,8,64,2048]{3,2,1,0:T(8,128)}, u32[]{:S(2)}) copy-start(f32[1,8,64,2048]{3,2,1,0:T(8,128)} %get-tuple-element.280) | copy-start | bytes 12582916 | tf_op jit(solution)/shard_map/while
  381.6 13.9 %copy-start = (f32[1,8,64,2048]{3,2,1,0:T(8,128)S(1)}, f32[1,8,64,2048]{3,2,1,0:T(8,128)}, u32[]{:S(2)}) copy-start(f32[1,8,64,2048]{3,2,1,0:T(8,128)} %get-tuple-element.281) | copy-start | bytes 12582916 | tf_op jit(solution)/shard_map/while
  381.6 13.9 %copy-start.1 = (f32[1,8,64,2048]{3,2,1,0:T(8,128)S(1)}, f32[1,8,64,2048]{3,2,1,0:T(8,128)}, u32[]{:S(2)}) copy-start(f32[1,8,64,2048]{3,2,1,0:T(8,128)} %get-tuple-element.280) | copy-start | bytes 12582916 | tf_op jit(solution)/shard_map/while
